TPU v7x, 256 devices: a whole 4x4x8 slice. The times are simulated.
256 devices in a mesh: patch: 32 (over z, x_hi, core), head: 8 (over y, x_lo).
Axes of the slice: x: 4 (x_hi: 2, x_lo: 2; x = x_hi * 2 + x_lo), y: 4, z: 8, core: 2. Of those that a mesh axis runs over, the one named last changes fastest.
Arguments:
- queries: bfloat16 [8192, 3072], P(('patch', 'head')), may hold values from -10 to 10
- fresh_keys: bfloat16 [8192, 3072], P('patch', 'head'), may hold values from -6 to 6
- fresh_values: bfloat16 [8192, 3072], P('patch', 'head'), may hold values from -6 to 6
- stale_keys: bfloat16 [8192, 3072], P(None, 'head'), may hold values from -6 to 6
- stale_values: bfloat16 [8192, 3072], P(None, 'head'), may hold values from -6 to 6
- key_basis: bfloat16 [24, 128, 64], P('head'), may hold values from -0.5 to 0.5
- value_basis: bfloat16 [24, 128, 64], P('head'), may hold values from -0.5 to 0.5
- owner_table: int32 [32], replicated, may hold values from 0 to 31, each once
- step_counter: int32 [32], replicated, may hold values from 0 to 3
Outputs:
- attended: bfloat16 [8192, 3072], P(('patch', 'head'))
Inputs may be any that keep to these rules, and one draw needn't show every extreme that they name: `owner_table`: a permutation of the patches.
All inputs are finite; a program needn't handle non-finite values.
Results may differ from a plain program's by a relative error of at most 0.0049.
The roundings to bfloat16 on the way count: a program that leaves them out, or rounds other values in their place, can miss the bound.
Values may be sent and summed in bfloat16 or wider, within the bound.
A program may use at most 192 MiB of HBM per device.

v0:
```python
import jax
import jax.numpy as jnp
from jax import lax
from jax.sharding import PartitionSpec as P


def code_rows(fresh_rows, old_rows, basis):
    row_count = fresh_rows.shape[0]
    head_count, head_width, code_rank = basis.shape
    delta = (fresh_rows.astype(jnp.float32) - old_rows.astype(jnp.float32)).reshape(
        row_count, head_count, head_width
    )
    return jnp.einsum(
        "shd,hdr->shr", delta, basis.astype(jnp.float32), precision=lax.Precision.HIGHEST
    ).astype(jnp.bfloat16)


def local(
    queries,
    fresh_keys,
    fresh_values,
    stale_keys,
    stale_values,
    key_basis,
    value_basis,
    owner_table,
    step_counter,
):
    head_count, head_width, code_rank = key_basis.shape
    score_scale = head_width ** (-0.5)
    patch_index = lax.axis_index("patch")
    patch_rows = fresh_keys.shape[0]
    patch_count = owner_table.shape[0]
    local_width = head_count * head_width
    local_queries = lax.all_to_all(
        queries, "head", split_axis=1, concat_axis=0, tiled=True
    ).reshape(patch_rows, head_count, head_width)
    blend_rate = 1.0 - jnp.exp2(-(step_counter.astype(jnp.float32) + 1.0))
    stale_key_blocks = stale_keys.reshape(patch_count, patch_rows, local_width)
    stale_value_blocks = stale_values.reshape(patch_count, patch_rows, local_width)
    own_block = lax.dynamic_slice_in_dim(owner_table, patch_index, 1)[0]
    own_old_keys = lax.dynamic_index_in_dim(stale_key_blocks, own_block, 0, keepdims=False)
    own_old_values = lax.dynamic_index_in_dim(stale_value_blocks, own_block, 0, keepdims=False)
    key_codes = code_rows(fresh_keys, own_old_keys, key_basis)
    value_codes = code_rows(fresh_values, own_old_values, value_basis)
    own_codes = jnp.concatenate((key_codes, value_codes), axis=1).reshape(
        patch_rows, 2 * head_count * code_rank
    )
    every_code = lax.all_gather(own_codes, "patch", axis=0, tiled=True)
    running_max = jnp.full((head_count, patch_rows), -1e30, jnp.float32)
    running_sum = jnp.zeros((head_count, patch_rows), jnp.float32)
    running_out = jnp.zeros((patch_rows, head_count, head_width), jnp.float32)
    row_count = every_code.shape[0]
    block_count = row_count // patch_rows
    first_block = 0 // patch_rows
    coded_parts = every_code.reshape(row_count, 2, head_count, code_rank)
    blend_part = blend_rate[:, None, None, None]
    block_ids = first_block + jnp.arange(block_count, dtype=jnp.int32)
    own_mask = (block_ids == patch_index)[:, None, None, None]

    def renew_side(stale_blocks, fresh_rows, basis, side_index):
        old_rows = (
            jnp.take(stale_blocks, owner_table, axis=0)
            .astype(jnp.float32)
            .reshape(block_count, patch_rows, head_count, head_width)
        )
        grown_rows = jnp.einsum(
            "shr,hdr->shd", coded_parts[:, side_index], basis, preferred_element_type=jnp.float32
        ).reshape(block_count, patch_rows, head_count, head_width)
        renewed = (old_rows + blend_part * grown_rows).astype(jnp.bfloat16)
        exact_rows = fresh_rows.reshape(1, patch_rows, head_count, head_width)
        return jnp.where(own_mask, exact_rows, renewed).reshape(row_count, head_count, head_width)

    key_rows = renew_side(stale_key_blocks, fresh_keys, key_basis, 0)
    value_rows = renew_side(stale_value_blocks, fresh_values, value_basis, 1)
    maxima = []
    sum_list = []
    outputs = []
    for head_id in range(head_count):
        scores = (
            jnp.einsum(
                "qd,kd->qk",
                local_queries[:, head_id],
                key_rows[:, head_id],
                preferred_element_type=jnp.float32,
            )
            * score_scale
        )
        new_max = jnp.maximum(running_max[head_id], jnp.max(scores, axis=1))
        exp_scores = jnp.exp(scores - new_max[:, None])
        factor = jnp.exp(running_max[head_id] - new_max)
        sum_list.append(running_sum[head_id] * factor + jnp.sum(exp_scores, axis=1))
        weighted = jnp.dot(
            exp_scores.astype(jnp.bfloat16),
            value_rows[:, head_id],
            preferred_element_type=jnp.float32,
        )
        outputs.append(running_out[:, head_id] * factor[:, None] + weighted)
        maxima.append(new_max)
    carry = (jnp.stack(maxima), jnp.stack(sum_list), jnp.stack(outputs, axis=1))
    final_max, final_sum, final_out = carry
    result = (
        (final_out / jnp.transpose(final_sum)[:, :, None])
        .astype(jnp.bfloat16)
        .reshape(patch_rows, head_count * head_width)
    )
    return lax.all_to_all(result, "head", split_axis=0, concat_axis=1, tiled=True)


def solution(mesh):
    in_specs = (
        P(("patch", "head"), None),
        P("patch", "head"),
        P("patch", "head"),
        P(None, "head"),
        P(None, "head"),
        P("head", None, None),
        P("head", None, None),
        P(),
        P(),
    )
    out_specs = P(("patch", "head"), None)
    return jax.shard_map(local, mesh=mesh, in_specs=in_specs, out_specs=out_specs, check_vma=False)
```

profile of v0, /device:TPU:1, one launch (start us, length us, event | category | flops | bytes accessed | tf_op | source)
XLA Modules:
  0.0 186.5 jit_solution(3877011375357641726)
XLA Ops:
  6.5 0.0 copy-start
  6.5 0.0 all-gather.2.cloned.1.call-start
  6.5 1.3 dynamic_slice.10
  9.7 1.3 convert_subtract_fusion
  11.0 0.2 copy.33
  11.2 0.2 copy.31
  11.4 1.1 fusion.38
  12.5 0.0 copy-done
  12.5 0.3 fusion.37
  12.8 0.7 pad_maximum_fusion
  13.5 0.0 all-gather.2.cloned.1.call-update
  13.5 1.6 copy.80
  15.1 5.9 %all-to-all-start = ((bf16[32,8,384]{2,0,1:T(8,128)(2,1)}), bf16[32,8,384]{2,0,1:T(8,128)(2,1)S(1)}, u32[]{:S(2)}, u32[]{:S(2)}) async-start(bf16[32,8,384]{2,0,1:T(8,128)(2,1)} %bitcast.117), calls=%async_computation | async-start | bytes 393216 | tf_op jit(solution)/shard_map/all_to_all | solution.py:35
  21.1 0.7 compare_select_fusion
  21.7 6.9 %gather_fusion = bf16[32,256,384]{2,1,0:T(8,128)(2,1)} fusion(bf16[32,256,384]{2,1,0:T(8,128)(2,1)} %bitcast.121, s32[1024]{0:T(1024)S(1)} %pad_clamp_fusion), kind=kCustom, calls=%fused_computation.clone | custom fusion | bytes 12583040 | tf_op jit(solution)/shard_map/jit(_take)/gather | solution.py:63
  28.6 0.0 copy-start.6
  28.6 0.0 copy-start.7
  28.6 7.1 %gather_fusion.1 = bf16[32,256,384]{2,1,0:T(8,128)(2,1)} fusion(bf16[32,256,384]{2,1,0:T(8,128)(2,1)} %bitcast.123, s32[1024]{0:T(1024)S(1)} %pad_clamp_fusion), kind=kCustom, calls=%fused_computation.1.clone | custom fusion | bytes 12583040 | tf_op jit(solution)/shard_map/jit(_take)/gather | solution.py:63
  35.7 0.0 copy-done.6
  35.7 0.0 copy-done.7
  35.7 0.0 copy-start.3
  35.7 0.0 copy-start.4
  35.7 12.3 %select_convert_fusion.1 = (f32[32,256,384]{2,1,0:T(8,128)}, f32[32,256,384]{2,1,0:T(8,128)}) fusion(bf16[32,256,384]{2,1,0:T(8,128)(2,1)} %gather_fusion, pred[32]{0:T(512)(128)(4,1)S(1)} %compare_and_fusion, bf16[32,256,384]{2,1,0:T(8,128)(2,1)} %gather_fusion.1), kind=kLoop, calls=%fused_computation.21 | loop fusion | flops 12582912 | bytes 37748768 | tf_op jit(solution)/shard_map/reshape | solution.py:65
  48.0 0.1 broadcast_bitcast_fusion
  48.1 0.0 copy-done.3
  48.1 0.1 copy.37
  48.2 0.0 copy-done.4
  48.3 0.1 copy.28
  48.4 0.2 copy.38
  48.6 19.0 %reshape.232 = f32[8192,3,128]{2,1,0:T(4,128)} reshape(f32[32,256,384]{2,1,0:T(8,128)} %get-tuple-element.16) | data formatting | bytes 25165824 | tf_op jit(solution)/shard_map/reshape | solution.py:65
  67.6 0.1 broadcast_in_dim.54
  67.7 0.2 copy.29
  67.8 19.1 %reshape.231 = f32[8192,3,128]{2,1,0:T(4,128)} reshape(f32[32,256,384]{2,1,0:T(8,128)} %get-tuple-element.15) | data formatting | bytes 25165824 | tf_op jit(solution)/shard_map/reshape | solution.py:65
  86.9 0.0 all-to-all-done
  86.9 0.1 reshape.197
  87.0 0.3 fusion.49
  87.3 28.2 %all-gather.2.cloned.1.call-done = bf16[8192,384]{0,1:T(8,128)(2,1)} async-done(((bf16[256,384]{0,1:T(8,128)(2,1)}), bf16[8192,384]{0,1:T(8,128)(2,1)}) %all-gather.2.cloned.1.call-update) | async-done | bytes 6291472 | tf_op jit(solution)/shard_map/all_gather | solution.py:49
  115.5 0.0 copy-start.2
  115.5 1.5 broadcast_in_dim.58
  117.0 1.2 copy-done.2
  118.3 11.0 %fusion.2 = bf16[8192,3,128]{2,0,1:T(8,128)(2,1)S(1)} fusion(bf16[8192,3,128]{2,0,1:T(8,128)(2,1)S(1)} %bitcast.119, bf16[3,128,64]{1,2,0:T(8,128)(2,1)S(1)} %copy-done, f32[8192,3,128]{2,1,0:T(4,128)} %reshape.231, f32[8192]{0:T(1024)S(1)} %bitcast.126, pred[8192]{0:T(1024)(128)(4,1)S(1)} %broadcast_in_dim.55, bf16[8192,2,3,64]{0,3,2,1:T(8,128)(2,1)S(1)} %bitcast.125), kind=kOutput, calls=%fused_computation.9 | convolution fusion | flops 415236096 | bytes 28401664 | tf_op jit(solution)/shard_map/shr,hdr->shd/dot_general | solution.py:67
  129.3 1.5 fusion.50
  130.8 1.2 fusion.8
  132.0 1.5 fusion.51
  133.6 0.0 copy-start.5
  133.6 1.2 fusion.6
  134.8 4.2 %broadcast_in_dim.61 = bf16[32,256,3,128]{3,1,0,2:T(8,128)(2,1)} broadcast(bf16[256,3,128]{2,0,1:T(8,128)(2,1)S(1)} %copy.38), dimensions={1,2,3} | broadcast | bytes 6488064 | tf_op jit(solution)/shard_map/jit(_where)/broadcast_in_dim | solution.py:72
  139.0 0.0 copy-done.5
  139.0 17.0 %fusion.3 = bf16[8192,3,128]{2,0,1:T(8,128)(2,1)} fusion(bf16[8192,3,128]{2,0,1:T(8,128)(2,1)} %bitcast.118, bf16[3,128,64]{1,2,0:T(8,128)(2,1)S(1)} %copy-done.5, f32[8192,3,128]{2,1,0:T(4,128)} %reshape.232, f32[8192]{0:T(1024)S(1)} %bitcast.127, pred[8192]{0:T(1024)(128)(4,1)S(1)} %broadcast_in_dim.55, bf16[8192,2,3,64]{0,3,2,1:T(8,128)(2,1)} %bitcast.124), kind=kOutput, calls=%fused_computation.10 | convolution fusion | flops 415236096 | bytes 32595968 | tf_op jit(solution)/shard_map/shr,hdr->shd/dot_general | solution.py:67
  156.0 3.2 %fusion.34 = f32[256,1,128]{2,0,1:T(8,128)S(1)} fusion(bf16[8192,3,128]{2,0,1:T(8,128)(2,1)} %fusion.3, f32[8192,256]{1,0:T(8,128)S(1)} %get-tuple-element.18, f32[256]{0:T(256)S(1)} %broadcast_maximum_fusion, f32[256]{0:T(256)S(1)} %get-tuple-element.14), kind=kOutput, calls=%fused_computation.43 | convolution fusion | flops 541097984 | bytes 10618880 | tf_op jit(solution)/shard_map/dot_general | solution.py:93
  159.2 3.2 %fusion.28 = f32[256,1,128]{2,0,1:T(8,128)S(1)} fusion(bf16[8192,3,128]{2,0,1:T(8,128)(2,1)} %fusion.3, f32[8192,256]{1,0:T(8,128)S(1)} %get-tuple-element.20, f32[256]{0:T(256)S(1)} %broadcast_maximum_fusion.1, f32[256]{0:T(256)S(1)} %get-tuple-element.12), kind=kOutput, calls=%fused_computation.41 | convolution fusion | flops 541097984 | bytes 10618880 | tf_op jit(solution)/shard_map/dot_general | solution.py:93
  162.4 1.5 fusion.52
  164.0 1.2 fusion.4
  165.2 0.0 copy-start.1
  165.2 3.2 %fusion.22 = f32[256,1,128]{2,0,1:T(8,128)S(1)} fusion(bf16[8192,3,128]{2,0,1:T(8,128)(2,1)} %fusion.3, f32[8192,256]{1,0:T(8,128)S(1)} %get-tuple-element.22, f32[256]{0:T(256)S(1)} %broadcast_maximum_fusion.2, f32[256]{0:T(256)S(1)} %get-tuple-element.10), kind=kOutput, calls=%fused_computation.39 | convolution fusion | flops 541097984 | bytes 10618880 | tf_op jit(solution)/shard_map/dot_general | solution.py:93
  168.4 0.2 fusion.39
  168.6 0.2 copy.41
  168.8 0.2 convert_element_type.82
  169.0 10.0 %all_to_all.32 = bf16[8,32,384]{2,1,0:T(8,128)(2,1)S(1)} all-to-all(bf16[8,32,384]{2,1,0:T(8,128)(2,1)S(1)} %convert_element_type.82), channel_id=1, replica_groups=mesh['patch'=32,'head'=8] {'head'}, dimensions={0} | all-to-all | bytes 393216 | tf_op jit(solution)/shard_map/all_to_all | solution.py:107
  178.9 0.7 copy.53
  179.6 0.0 copy-done.1
  (13 shorter events, 0.1 us)
Async XLA Ops:
  6.5 5.9 %copy-start = (bf16[3,128,64]{1,2,0:T(8,128)(2,1)S(1)}, bf16[3,128,64]{1,2,0:T(8,128)(2,1)}, u32[]{:S(2)}) copy-start(bf16[3,128,64]{1,2,0:T(8,128)(2,1)} %param.16) | copy-start | bytes 147460
  6.5 109.0 %all-gather.2.cloned.1.call-start = ((), (), s32[]{:S(2)}) async-start(), calls=%async_computation.2 | async-start | bytes 6488064 | tf_op jit(solution)/shard_map/all_gather | solution.py:49
  15.1 71.8 %all-to-all-start = ((bf16[32,8,384]{2,0,1:T(8,128)(2,1)}), bf16[32,8,384]{2,0,1:T(8,128)(2,1)S(1)}, u32[]{:S(2)}, u32[]{:S(2)}) async-start(bf16[32,8,384]{2,0,1:T(8,128)(2,1)} %bitcast.117), calls=%async_computation | async-start | bytes 393216 | tf_op jit(solution)/shard_map/all_to_all | solution.py:35
  28.6 7.1 %copy-start.6 = (s32[32]{0:T(128)S(1)}, s32[32]{0:T(128)}, u32[]{:S(2)}) copy-start(s32[32]{0:T(128)} %param.18) | copy-start | bytes 388
  28.6 7.1 %copy-start.7 = (s32[32]{0:T(128)S(1)}, s32[32]{0:T(128)}, u32[]{:S(2)}) copy-start(s32[32]{0:T(128)} %param.19) | copy-start | bytes 388
  35.7 12.4 %copy-start.3 = (bf16[256,384]{1,0:T(8,128)(2,1)S(1)}, bf16[256,384]{1,0:T(8,128)(2,1)}, u32[]{:S(2)}) copy-start(bf16[256,384]{1,0:T(8,128)(2,1)} %param.13) | copy-start | bytes 589828
  35.7 12.5 %copy-start.4 = (bf16[256,384]{1,0:T(8,128)(2,1)S(1)}, bf16[256,384]{1,0:T(8,128)(2,1)}, u32[]{:S(2)}) copy-start(bf16[256,384]{1,0:T(8,128)(2,1)} %param.12) | copy-start | bytes 589828
  115.5 2.8 %copy-start.2 = (bf16[8192,384]{0,1:T(8,128)(2,1)S(1)}, bf16[8192,384]{0,1:T(8,128)(2,1)}, u32[]{:S(2)}) copy-start(bf16[8192,384]{0,1:T(8,128)(2,1)} %all-gather.2.cloned.1.call-done) | copy-start | bytes 18874372
  133.6 5.4 %copy-start.5 = (bf16[3,128,64]{1,2,0:T(8,128)(2,1)S(1)}, bf16[3,128,64]{1,2,0:T(8,128)(2,1)}, u32[]{:S(2)}) copy-start(bf16[3,128,64]{1,2,0:T(8,128)(2,1)} %param.17) | copy-start | bytes 147460
  165.2 14.5 %copy-start.1 = (bf16[3,128,64]{1,2,0:T(8,128)(2,1)S(1)}, bf16[3,128,64]{1,2,0:T(8,128)(2,1)}, u32[]{:S(2)}) copy-start(bf16[3,128,64]{1,2,0:T(8,128)(2,1)} %param.16) | copy-start | bytes 147460
Sparse Core Ops, SparseCore 0:
  13.6 101.8 all-gather.1
where the time goes:
time: 188 us; the launch traced here: 186 us
  local copies, waits for them, and re-layouts  64.4 us (34%)
  matrix products  43.6 us (23%)
  waiting for transfers between devices  28.2 us (15%)
  other arithmetic  18.7 us (10%)
  between operations  15.6 us (8%)
  blocking collectives  9.96 us (5%)
  starting transfers between devices  5.95 us (3%)
    reshape x2, local copies, waits for them, and re-layouts, renew_side(): old_rows = jnp.take(stale_blocks, owner_table, axis=0).astype(jnp.float32...  38.1 us
    all_gather x1, waiting for transfers between devices, local(): every_code = lax.all_gather(own_codes, 'patch', axis=0, tiled=True)  28.2 us
    dot_general x2, matrix products, renew_side(): jnp.einsum('shr,hdr->shd', coded_parts[:, side_index], basis, preferred_e...  28 us
    gather x2, local copies, waits for them, and re-layouts, renew_side(): jnp.take(stale_blocks, owner_table, axis=0).astype(jnp.float32)  14 us
    reshape x1, other arithmetic, renew_side(): old_rows = jnp.take(stale_blocks, owner_table, axis=0).astype(jnp.float32...  12.3 us
    all_to_all x1, blocking collectives, local(): lax.all_to_all(result, 'head', split_axis=0, concat_axis=1, tiled=True)  9.96 us
    dot_general x3, matrix products, local(): jnp.dot(exp_scores.astype(jnp.bfloat16), value_rows[:, head_id], preferre...  9.68 us
    broadcast_in_dim x6, local copies, waits for them, and re-layouts, renew_side(): jnp.where(own_mask, exact_rows, renewed)  6.16 us
  transfers between devices with their start and end apart: 2, of which 1 were waited for; matrix products, arithmetic and copies ran while one was open for 36% of the time, Pallas kernels for 0%

commit v1 on v0

v1 whole, which is shorter than its diff:
```python
import functools
import math

import jax
import jax.numpy as jnp
from jax import lax
from jax.experimental import pallas as pl
from jax.experimental.pallas import tpu as pltpu
from jax.sharding import PartitionSpec as P

MESH = pl.DeviceIdType.MESH
F32 = jnp.float32
BF16 = jnp.bfloat16
LOG2E = math.log2(math.e)
LANES = 128


def across(a, b):
    return lax.dot_general(a, b, (((1,), (1,)), ((), ())), preferred_element_type=F32)


def kernel(
    dims,
    owner_ref,
    step_ref,
    queries_ref,
    fresh_k_ref,
    fresh_v_ref,
    stale_k_ref,
    stale_v_ref,
    basis_k_ref,
    basis_v_ref,
    out_ref,
    stale,
    fresh,
    basis,
    qbuf,
    codes,
    keys,
    values,
    own_keys,
    own_values,
    acc,
    best,
    part_out,
    part_stat,
    got_out,
    got_stat,
    sum_out,
    sum_stat,
    final_out,
    final_stat,
    load_sem,
    q_send,
    q_recv,
    qc_sem,
    ring_send,
    ring_recv,
    part_send,
    part_recv,
    final_send,
    final_recv,
):
    heads, nz, nh, rows = dims
    width = heads * LANES
    small = rows // nh
    per_group = LANES // small
    groups = rows // LANES
    scale = LOG2E / math.sqrt(LANES)
    half = rows // 2

    patch = lax.axis_index("patch")
    head = lax.axis_index("head")
    core = lax.rem(patch, 2)
    xh = lax.rem(patch // 2, 2)
    z = patch // 4

    def patch_of(z_, x_, c_):
        return (z_ * 2 + x_) * 2 + c_

    partner = (patch_of(z, xh, 1 - core), head)
    right = (patch_of(lax.rem(z + 1, nz), xh, core), head)
    left = (patch_of(lax.rem(z + nz - 1, nz), xh, core), head)

    def plane(t):
        tx = lax.rem(xh + t // nh, 2)
        th = lax.rem(head + lax.rem(t, nh), nh)
        return tx, th

    loads = []
    for i, src in enumerate((fresh_k_ref, fresh_v_ref)):
        loads.append(pltpu.make_async_copy(src, fresh.at[i], load_sem.at[i]))
    for j in range(heads):
        for i, src in enumerate((stale_k_ref, stale_v_ref)):
            loads.append(
                pltpu.make_async_copy(
                    src.at[:, :, j * LANES : (j + 1) * LANES],
                    stale[2 * j + i],
                    load_sem.at[2 + 2 * j + i],
                )
            )
    for load in loads:
        load.start()

    barrier = pltpu.get_barrier_semaphore()
    for device in (partner, right, left):
        pl.semaphore_signal(barrier, inc=1, device_id=device, device_id_type=MESH)

    @pl.loop(1, 2 * nh)
    def _(t):
        tx, th = plane(t)
        pl.semaphore_signal(
            barrier, inc=1, device_id=(patch_of(z, tx, core), th), device_id_type=MESH
        )

    rank = basis_k_ref.shape[1]
    blank = jnp.zeros((rank, LANES), BF16)
    for j in range(heads):
        basis[j, :rank, :LANES] = basis_k_ref[j]
        basis[j, :rank, LANES:] = blank
        basis[j, rank:, :LANES] = blank
        basis[j, rank:, LANES:] = basis_v_ref[j]
    ones = jnp.ones(values.shape[:3] + (LANES,), BF16)
    values[:, :, :, LANES:] = ones
    own_values[:, :, LANES:] = ones[:, 0]
    sum_stat[...] = jnp.zeros(sum_stat.shape, F32)

    pl.semaphore_wait(barrier, 3 + 2 * nh - 1)

    def q_copy(t):
        tx, th = plane(t)
        return pltpu.make_async_remote_copy(
            src_ref=queries_ref.at[:, pl.ds(pl.multiple_of(th * width, LANES), width)],
            dst_ref=qbuf.at[
                pl.ds(pl.multiple_of((t // nh) * rows + head * small, small), small), :
            ],
            send_sem=q_send.at[t],
            recv_sem=q_recv.at[t],
            device_id=(patch_of(z, tx, core), th),
            device_id_type=MESH,
        )

    q_self = pltpu.make_async_copy(
        queries_ref.at[:, pl.ds(pl.multiple_of(head * width, LANES), width)],
        qbuf.at[pl.ds(pl.multiple_of(head * small, small), small), :],
        q_recv.at[0],
    )
    q_self.start()

    @pl.loop(1, 2 * nh)
    def _(t):
        q_copy(t).start()

    def ring_copy(j, s, way):
        slot = lax.rem(z + nz - s, nz) if way == 0 else lax.rem(z + s, nz)
        ref = codes.at[j, slot]
        if s == nz // 2 - 1:
            ref = ref.at[pl.ds(way * half, half)]
        return pltpu.make_async_remote_copy(
            src_ref=ref,
            dst_ref=ref,
            send_sem=ring_send.at[j, s, way],
            recv_sem=ring_recv.at[j, s, way],
            device_id=right if way == 0 else left,
            device_id_type=MESH,
        )

    def old_rows(j, side, patch_id):
        return stale[2 * j + side][owner_ref[patch_id]].astype(F32)

    def encode(j):
        lanes = slice(j * LANES, (j + 1) * LANES)
        delta = jnp.concatenate(
            [fresh[i, :, lanes].astype(F32) - old_rows(j, i, patch) for i in range(2)], axis=1
        )
        first = delta.astype(BF16)
        rest = delta - first.astype(F32)
        second = rest.astype(BF16)
        third = (rest - second.astype(F32)).astype(BF16)
        total = across(third, basis[j])
        total += across(second, basis[j])
        total += across(first, basis[j])
        codes[j, z] = total.astype(BF16)
        for way in range(2):
            ring_copy(j, 0, way).start()

    def decode(j, slot, chunk, side):
        patch_id = patch_of(slot, xh, core)
        count = step_ref[patch_id].astype(F32)
        pairs = count * (count - 1.0)
        keep = 0.5 - 0.25 * count + 0.0625 * pairs - (pairs * (count - 2.0)) * (1 / 6) * 0.0625
        blend = 1.0 - keep
        grown = jnp.dot(codes[j, slot], basis[j], preferred_element_type=F32)
        new_k = (old_rows(j, 0, patch_id) + blend * grown[:, :LANES]).astype(BF16)
        new_v = (old_rows(j, 1, patch_id) + blend * grown[:, LANES:]).astype(BF16)
        at = slice(side * rows, (side + 1) * rows)
        keys[j, chunk, at] = new_k
        values[j, chunk, at, :LANES] = new_v
        if chunk == 0 and side == 1:
            own_keys[j, at] = new_k
            own_values[j, at, :LANES] = new_v

    def arrive(j, s):
        for way in range(2):
            ring_copy(j, s, way).wait_recv()
        if s < nz // 2 - 1:
            for way in range(2):
                ring_copy(j, s + 1, way).start()
            decode(j, lax.rem(z + nz - 1 - s, nz), s, 1)
            decode(j, lax.rem(z + 1 + s, nz), s + 1, 0)
        else:
            decode(j, lax.rem(z + nz // 2, nz), s, 1)

    def part(j, at, k, v, first):
        q = qbuf[at, j * LANES : (j + 1) * LANES]
        scores = across(q, k)
        top = jnp.max(scores, axis=1, keepdims=True)
        if first:
            now = jnp.broadcast_to(top, (q.shape[0], LANES))
        else:
            before = best[j, at]
            now = jnp.maximum(before, top)
        weights = jnp.exp2(scores * scale - now[:, :1] * scale).astype(BF16)
        added = jnp.dot(weights, v, preferred_element_type=F32)
        if first:
            acc[j, at] = added
        else:
            factor = jnp.exp2((before - now) * scale)
            acc[j, at, :LANES] = acc[j, at, :LANES] * factor + added[:, :LANES]
            acc[j, at, LANES:] = acc[j, at, LANES:] * factor + added[:, LANES:]
        best[j, at] = now

    def attend(j, chunk):
        if chunk == 0:
            part(j, slice(0, rows), own_keys[j], own_values[j], True)
            part(j, slice(rows, 4 * rows), keys[j, 0], values[j, 0], True)
        else:
            part(j, slice(0, 4 * rows), keys[j, chunk], values[j, chunk], False)

    row_id = lax.broadcasted_iota(jnp.int32, (LANES, LANES), 0)
    lane_id = lax.broadcasted_iota(jnp.int32, (LANES, LANES), 1)
    diagonal = row_id == lane_id

    def pack(column):
        return jnp.sum(jnp.where(diagonal, column, 0.0), axis=0, keepdims=True)

    def unpack(line):
        return jnp.sum(
            jnp.where(diagonal, jnp.broadcast_to(line, (LANES, LANES)), 0.0),
            axis=1,
            keepdims=True,
        )

    def local_result(j, at):
        total = acc[j, at, LANES:]
        level = best[j, at] * scale + jnp.log(total) * LOG2E
        return acc[j, at, :LANES] / total, level

    def part_copy(j, which):
        src, dst = ((part_out, got_out), (part_stat, got_stat))[which]
        return pltpu.make_async_remote_copy(
            src_ref=src.at[j],
            dst_ref=dst.at[j],
            send_sem=part_send.at[j, which],
            recv_sem=part_recv.at[j, which],
            device_id=partner,
            device_id_type=MESH,
        )

    def share(j):
        lines = []
        for g in range(2 * groups):
            result, level = local_result(j, pl.ds(2 * rows + g * LANES, LANES))
            part_out[j, g * LANES : (g + 1) * LANES] = result.astype(BF16)
            lines.append(pack(level))
        pad = part_stat.shape[1] - len(lines)
        if pad:
            lines.append(jnp.zeros((pad, LANES), F32))
        part_stat[j] = jnp.concatenate(lines, axis=0)
        for which in range(2):
            part_copy(j, which).start()

    def mix(result_a, level_a, result_b, level_b):
        share_a = 1.0 / (1.0 + jnp.exp2(level_b - level_a))
        return result_a * share_a + result_b * (1.0 - share_a)

    def merge(j):
        for which in range(2):
            part_copy(j, which).wait_recv()
        for g in range(2 * groups):
            at = slice(g * LANES, (g + 1) * LANES)
            result, level = local_result(j, pl.ds(g * LANES, LANES))
            other = got_out[j, at].astype(F32)
            other_level = unpack(got_stat[j, g : g + 1])
            mixed = mix(result, level, other, other_level)
            sum_out[at, j * LANES : (j + 1) * LANES] = mixed.astype(BF16)
            top = jnp.maximum(level, other_level)
            low = jnp.minimum(level, other_level)
            joint = top + jnp.log(1.0 + jnp.exp2(low - top)) * LOG2E
            sum_stat[g, j : j + 1] = pack(joint)

    def final_refs(t, th):
        src = sum_out.at[
            pl.ds(pl.multiple_of((t // nh) * rows + th * small, small), small), :
        ]
        dst = final_out.at[t // nh, :, pl.ds(pl.multiple_of(head * width, LANES), width)]
        stat_src = sum_stat.at[(t // nh) * groups + th // per_group]
        stat_dst = final_stat.at[t // nh, head]
        return (src, dst), (stat_src, stat_dst)

    def final_copy(t, which):
        tx, th = plane(t)
        src, dst = final_refs(t, th)[which]
        return pltpu.make_async_remote_copy(
            src_ref=src,
            dst_ref=dst,
            send_sem=final_send.at[which, t],
            recv_sem=final_recv.at[which, t],
            device_id=(patch_of(z, tx, core), th),
            device_id_type=MESH,
        )

    for load in loads[:2]:
        load.wait()
    for j in range(heads):
        loads[2 + 2 * j].wait()
        loads[3 + 2 * j].wait()
        encode(j)

    q_self.wait()

    @pl.loop(1, 2 * nh)
    def _(t):
        q_copy(t).wait_recv()

    q_cross = pltpu.make_async_remote_copy(
        src_ref=qbuf.at[pl.ds(0, 2 * rows)],
        dst_ref=qbuf.at[pl.ds(2 * rows, 2 * rows)],
        send_sem=qc_sem.at[0],
        recv_sem=qc_sem.at[1],
        device_id=partner,
        device_id_type=MESH,
    )
    q_cross.start()

    for j in range(heads):
        own_keys[j, :rows] = fresh[0, :, j * LANES : (j + 1) * LANES]
        own_values[j, :rows, :LANES] = fresh[1, :, j * LANES : (j + 1) * LANES]
        decode(j, z, 0, 0)
    for j in range(heads):
        arrive(j, 0)
    q_cross.wait_recv()

    steps = nz // 2
    items = [(s, j) for s in range(steps) for j in range(heads)]
    seen = heads
    for i, (s, j) in enumerate(items):
        ahead = 2 if s == 0 else 1
        while seen <= i or (seen < i + ahead and seen < 2 * heads):
            arrive(items[seen][1], items[seen][0])
            seen += 1
        attend(j, s)
        if s == steps - 1:
            share(j)

    for j in range(heads):
        merge(j)

    (src, dst), (stat_src, stat_dst) = final_refs(0, head)
    final_self = [
        pltpu.make_async_copy(src, dst, final_recv.at[0, 0]),
        pltpu.make_async_copy(stat_src, stat_dst, final_recv.at[1, 0]),
    ]
    for copy in final_self:
        copy.start()

    @pl.loop(1, 2 * nh)
    def _(t):
        for which in range(2):
            final_copy(t, which).start()

    for copy in final_self:
        copy.wait()

    @pl.loop(1, 2 * nh)
    def _(t):
        for which in range(2):
            final_copy(t, which).wait_recv()

    lane = lax.broadcasted_iota(jnp.int32, (small, LANES), 1)
    row = lax.broadcasted_iota(jnp.int32, (small, LANES), 0)
    mine = lane == row + lax.rem(head, per_group) * small

    def pick(line):
        return jnp.sum(
            jnp.where(mine, jnp.broadcast_to(line, (small, LANES)), 0.0), axis=1, keepdims=True
        )

    @pl.loop(0, nh)
    def _(g):
        for j in range(heads):
            lanes = pl.ds(pl.multiple_of((g * heads + j) * LANES, LANES), LANES)
            results = [final_out[x, :, lanes].astype(F32) for x in range(2)]
            levels = [pick(final_stat[x, g, j : j + 1]) for x in range(2)]
            mixed = mix(results[0], levels[0], results[1], levels[1])
            out_ref[:, lanes] = mixed.astype(BF16)

    @pl.loop(1, 2 * nh)
    def _(t):
        q_copy(t).wait_send()
        for which in range(2):
            final_copy(t, which).wait_send()

    q_cross.wait_send()
    for j in range(heads):
        for s in range(steps):
            for way in range(2):
                ring_copy(j, s, way).wait_send()
        for which in range(2):
            part_copy(j, which).wait_send()


def make_local(nz, nh):
    def local(
        queries,
        fresh_keys,
        fresh_values,
        stale_keys,
        stale_values,
        key_basis,
        value_basis,
        owner_table,
        step_counter,
    ):
        heads = key_basis.shape[0]
        rows = fresh_keys.shape[0]
        small = queries.shape[0]
        width = heads * LANES
        seq = stale_keys.shape[0]
        chunks = nz // 2
        groups = rows // LANES
        smem = pl.BlockSpec(memory_space=pltpu.SMEM)
        hbm = pl.BlockSpec(memory_space=pl.ANY)
        vmem = pl.BlockSpec(memory_space=pltpu.VMEM)
        dma = pltpu.SemaphoreType.DMA
        scratch = [
            [pltpu.VMEM((seq // rows, rows, LANES), BF16) for _ in range(2 * heads)],
            pltpu.VMEM((2, rows, width), BF16),
            pltpu.VMEM((heads, LANES, 2 * LANES), BF16),
            pltpu.VMEM((4 * rows, width), BF16),
            pltpu.VMEM((heads, nz, rows, LANES), BF16),
            pltpu.VMEM((heads, chunks, 2 * rows, LANES), BF16),
            pltpu.VMEM((heads, chunks, 2 * rows, 2 * LANES), BF16),
            pltpu.VMEM((heads, 2 * rows, LANES), BF16),
            pltpu.VMEM((heads, 2 * rows, 2 * LANES), BF16),
            pltpu.VMEM((heads, 4 * rows, 2 * LANES), F32),
            pltpu.VMEM((heads, 4 * rows, LANES), F32),
            pltpu.VMEM((heads, 2 * rows, LANES), BF16),
            pltpu.VMEM((heads, 8, LANES), F32),
            pltpu.VMEM((heads, 2 * rows, LANES), BF16),
            pltpu.VMEM((heads, 8, LANES), F32),
            pltpu.VMEM((2 * rows, width), BF16),
            pltpu.VMEM((2 * groups, 8, LANES), F32),
            pltpu.VMEM((2, small, nh * width), BF16),
            pltpu.VMEM((2, nh, 8, LANES), F32),
            dma((2 + 2 * heads,)),
            dma((2 * nh,)),
            dma((2 * nh,)),
            dma((2,)),
            dma((heads, chunks, 2)),
            dma((heads, chunks, 2)),
            dma((heads, 2)),
            dma((heads, 2)),
            dma((2, 2 * nh)),
            dma((2, 2 * nh)),
        ]
        return pl.pallas_call(
            functools.partial(kernel, (heads, nz, nh, rows)),
            out_shape=jax.ShapeDtypeStruct((small, nh * width), BF16),
            in_specs=[smem, smem, hbm, hbm, hbm, hbm, hbm, vmem, vmem],
            out_specs=vmem,
            scratch_shapes=scratch,
            compiler_params=pltpu.CompilerParams(
                collective_id=0, has_side_effects=True, vmem_limit_bytes=48 << 20
            ),
            name="patch_attention",
        )(
            owner_table,
            step_counter,
            queries,
            fresh_keys,
            fresh_values,
            stale_keys.reshape(seq // rows, rows, width),
            stale_values.reshape(seq // rows, rows, width),
            jnp.swapaxes(key_basis, 1, 2),
            jnp.swapaxes(value_basis, 1, 2),
        )

    return local


def solution(mesh):
    in_specs = (
        P(("patch", "head"), None),
        P("patch", "head"),
        P("patch", "head"),
        P(None, "head"),
        P(None, "head"),
        P("head", None, None),
        P("head", None, None),
        P(),
        P(),
    )
    out_specs = P(("patch", "head"), None)
    local = make_local(mesh.shape["patch"] // 4, mesh.shape["head"])
    return jax.shard_map(local, mesh=mesh, in_specs=in_specs, out_specs=out_specs, check_vma=False)
```

time: 188 us -> 58.4 us (0.31)
  local copies, waits for them, and re-layouts: 64.4 us -> 6.36 us
  Pallas kernels: 0 us -> 51.8 us
  matrix products: 43.6 us -> 0 us
  waiting for transfers between devices: 28.2 us -> 0 us
  other arithmetic: 18.7 us -> 0 us
  between operations: 15.6 us -> 0.02 us
  blocking collectives: 9.96 us -> 0 us
  starting transfers between devices: 5.95 us -> 0 us
    pallas_call x0 -> x1, Pallas kernels: none -> 51.8 us  [local(): pl.pallas_call(functools.partial(kernel, (heads, nz, nh, rows)), out_shap...]
    dot_general x10 -> x0, matrix products: 43.6 us -> none  [the longest x2 28 us: renew_side(): jnp.einsum('shr,hdr->shd', coded_parts[:, side_index], basis, preferred_e...]
    reshape x3 -> x0, local copies, waits for them, and re-layouts: 38.1 us -> none  [the longest x2 38.1 us: renew_side(): old_rows = jnp.take(stale_blocks, owner_table, axis=0).astype(jnp.float32...]
    all_gather x1 -> x0, waiting for transfers between devices: 28.2 us -> none  [local(): every_code = lax.all_gather(own_codes, 'patch', axis=0, tiled=True)]
    gather x2 -> x0, local copies, waits for them, and re-layouts: 14 us -> none  [renew_side(): jnp.take(stale_blocks, owner_table, axis=0).astype(jnp.float32)]
    reshape x1 -> x0, other arithmetic: 12.3 us -> none  [renew_side(): old_rows = jnp.take(stale_blocks, owner_table, axis=0).astype(jnp.float32...]
    all_to_all x1 -> x0, blocking collectives: 9.96 us -> none  [local(): lax.all_to_all(result, 'head', split_axis=0, concat_axis=1, tiled=True)]
    broadcast_in_dim x6 -> x0, local copies, waits for them, and re-layouts: 6.16 us -> none  [renew_side(): jnp.where(own_mask, exact_rows, renewed)]
  transfers between devices with their start and end apart: 2 -> 0, of which waited for: 1 -> 0; matrix products, arithmetic and copies ran while one was open for 36% -> 0% of each run, Pallas kernels for 0% -> 0%
where the time goes in v1:
time: 58.4 us; the launch traced here: 58.2 us
  Pallas kernels  51.8 us (89%)
  local copies, waits for them, and re-layouts  6.36 us (11%)
    pallas_call x1, Pallas kernels, local(): pl.pallas_call(functools.partial(kernel, (heads, nz, nh, rows)), out_shap...  51.8 us
    unnamed x15, local copies, waits for them, and re-layouts  6.36 us

profile of v1, /device:TPU:1, one launch (start us, length us, event | category | flops | bytes accessed | tf_op | source)
XLA Modules:
  0.0 58.2 jit_solution(8207025926160971370)
XLA Ops:
  0.0 0.0 copy-start
  0.0 0.9 %copy-done = bf16[32,3072]{1,0:T(8,128)(2,1)S(1)} copy-done((bf16[32,3072]{1,0:T(8,128)(2,1)S(1)}, bf16[32,3072]{1,0:T(8,128)(2,1)}, u32[]{:S(2)}) %copy-start) | copy-done | bytes 196632
  0.9 0.0 copy-start.1
  0.9 0.9 %copy-done.1 = bf16[256,384]{1,0:T(8,128)(2,1)S(1)} copy-done((bf16[256,384]{1,0:T(8,128)(2,1)S(1)}, bf16[256,384]{1,0:T(8,128)(2,1)}, u32[]{:S(2)}) %copy-start.1) | copy-done | bytes 196632
  1.9 0.0 copy-start.2
  1.9 0.9 %copy-done.2 = bf16[256,384]{1,0:T(8,128)(2,1)S(1)} copy-done((bf16[256,384]{1,0:T(8,128)(2,1)S(1)}, bf16[256,384]{1,0:T(8,128)(2,1)}, u32[]{:S(2)}) %copy-start.2) | copy-done | bytes 196632
  2.8 0.0 copy-start.3
  2.8 0.8 %copy-done.3 = bf16[3,128,64]{1,2,0:T(8,128)(2,1)S(1)} copy-done((bf16[3,128,64]{1,2,0:T(8,128)(2,1)S(1)}, bf16[3,128,64]{1,2,0:T(8,128)(2,1)}, u32[]{:S(2)}) %copy-start.3) | copy-done | bytes 49176
  3.6 0.0 copy-start.4
  3.6 0.8 %copy-done.4 = bf16[3,128,64]{1,2,0:T(8,128)(2,1)S(1)} copy-done((bf16[3,128,64]{1,2,0:T(8,128)(2,1)S(1)}, bf16[3,128,64]{1,2,0:T(8,128)(2,1)}, u32[]{:S(2)}) %copy-start.4) | copy-done | bytes 49176
  4.4 0.0 copy-start.5
  4.4 0.7 %copy-done.5 = s32[32]{0:T(128)S(1)} copy-done((s32[32]{0:T(128)S(1)}, s32[32]{0:T(128)}, u32[]{:S(2)}) %copy-start.5) | copy-done | bytes 152
  5.0 0.0 copy-start.6
  5.0 0.7 %copy-done.6 = s32[32]{0:T(128)S(1)} copy-done((s32[32]{0:T(128)S(1)}, s32[32]{0:T(128)}, u32[]{:S(2)}) %copy-start.6) | copy-done | bytes 152
  5.7 51.8 %patch_attention.1 = bf16[32,3072]{1,0:T(8,128)(2,1)S(1)} custom-call(s32[32]{0:T(128)S(1)} %copy-done.5, s32[32]{0:T(128)S(1)} %copy-done.6, bf16[32,3072]{1,0:T(8,128)(2,1)S(1)} %copy-done, bf16[256,384]{1,0:T(8,128)(2,1)S(1)} %copy-done.1, bf16[256,384]{1,0:T(8,128)(2,1)S(1)} %copy-done.2, bf16[32,256,384]{2,1,0:T(8,128)(2,1)} %bitcast.6, ...), custom_call_target="tpu_custom_call" | custom-call | tf_op jit(solution)/shard_map/patch_attention/pallas_call | solution.py:477
  57.5 0.7 %copy.11 = bf16[32,3072]{1,0:T(8,128)(2,1)} copy(bf16[32,3072]{1,0:T(8,128)(2,1)S(1)} %patch_attention.1) | data formatting | bytes 393216
Async XLA Ops:
  0.0 0.9 %copy-start = (bf16[32,3072]{1,0:T(8,128)(2,1)S(1)}, bf16[32,3072]{1,0:T(8,128)(2,1)}, u32[]{:S(2)}) copy-start(bf16[32,3072]{1,0:T(8,128)(2,1)} %queries_ref.1) | copy-start | bytes 589828
  0.9 0.9 %copy-start.1 = (bf16[256,384]{1,0:T(8,128)(2,1)S(1)}, bf16[256,384]{1,0:T(8,128)(2,1)}, u32[]{:S(2)}) copy-start(bf16[256,384]{1,0:T(8,128)(2,1)} %fresh_k_ref.1) | copy-start | bytes 589828
  1.9 0.9 %copy-start.2 = (bf16[256,384]{1,0:T(8,128)(2,1)S(1)}, bf16[256,384]{1,0:T(8,128)(2,1)}, u32[]{:S(2)}) copy-start(bf16[256,384]{1,0:T(8,128)(2,1)} %fresh_v_ref.1) | copy-start | bytes 589828
  2.8 0.8 %copy-start.3 = (bf16[3,128,64]{1,2,0:T(8,128)(2,1)S(1)}, bf16[3,128,64]{1,2,0:T(8,128)(2,1)}, u32[]{:S(2)}) copy-start(bf16[3,128,64]{1,2,0:T(8,128)(2,1)} %param.14) | copy-start | bytes 147460
  3.6 0.8 %copy-start.4 = (bf16[3,128,64]{1,2,0:T(8,128)(2,1)S(1)}, bf16[3,128,64]{1,2,0:T(8,128)(2,1)}, u32[]{:S(2)}) copy-start(bf16[3,128,64]{1,2,0:T(8,128)(2,1)} %param.15) | copy-start | bytes 147460
  4.4 0.7 %copy-start.5 = (s32[32]{0:T(128)S(1)}, s32[32]{0:T(128)}, u32[]{:S(2)}) copy-start(s32[32]{0:T(128)} %owner_ref.1) | copy-start | bytes 388
  5.0 0.7 %copy-start.6 = (s32[32]{0:T(128)S(1)}, s32[32]{0:T(128)}, u32[]{:S(2)}) copy-start(s32[32]{0:T(128)} %step_ref.1) | copy-start | bytes 388

commit v2 on v1

--- a/solution.py
+++ b/solution.py
@@ -31,6 +31,9 @@
     basis_k_ref,
     basis_v_ref,
     out_ref,
+    owner_smem,
+    step_smem,
+    basis_in,
     stale,
     fresh,
     basis,
@@ -67,7 +70,6 @@
     per_group = LANES // small
     groups = rows // LANES
     scale = LOG2E / math.sqrt(LANES)
-    half = rows // 2
 
     patch = lax.axis_index("patch")
     head = lax.axis_index("head")
@@ -99,7 +101,18 @@
                     load_sem.at[2 + 2 * j + i],
                 )
             )
-    for load in loads:
+    small_loads = [
+        pltpu.make_async_copy(src, dst, load_sem.at[2 + 2 * heads + i])
+        for i, (src, dst) in enumerate(
+            (
+                (owner_ref, owner_smem),
+                (step_ref, step_smem),
+                (basis_k_ref, basis_in.at[0]),
+                (basis_v_ref, basis_in.at[1]),
+            )
+        )
+    ]
+    for load in small_loads + loads:
         load.start()
 
     barrier = pltpu.get_barrier_semaphore()
@@ -113,60 +126,101 @@
             barrier, inc=1, device_id=(patch_of(z, tx, core), th), device_id_type=MESH
         )
 
+    for load in small_loads:
+        load.wait()
     rank = basis_k_ref.shape[1]
     blank = jnp.zeros((rank, LANES), BF16)
     for j in range(heads):
-        basis[j, :rank, :LANES] = basis_k_ref[j]
+        basis[j, :rank, :LANES] = basis_in[0, j]
         basis[j, :rank, LANES:] = blank
         basis[j, rank:, :LANES] = blank
-        basis[j, rank:, LANES:] = basis_v_ref[j]
-    ones = jnp.ones(values.shape[:3] + (LANES,), BF16)
-    values[:, :, :, LANES:] = ones
-    own_values[:, :, LANES:] = ones[:, 0]
-    sum_stat[...] = jnp.zeros(sum_stat.shape, F32)
-
+        basis[j, rank:, LANES:] = basis_in[1, j]
     pl.semaphore_wait(barrier, 3 + 2 * nh - 1)
 
-    def q_copy(t):
+    def q_lanes(th, j):
+        return pl.ds(pl.multiple_of(th * width + j * LANES, LANES), LANES)
+
+    def q_copy(t, j):
         tx, th = plane(t)
+        start = pl.multiple_of((t // nh) * rows + head * small, small)
         return pltpu.make_async_remote_copy(
-            src_ref=queries_ref.at[:, pl.ds(pl.multiple_of(th * width, LANES), width)],
-            dst_ref=qbuf.at[
-                pl.ds(pl.multiple_of((t // nh) * rows + head * small, small), small), :
-            ],
-            send_sem=q_send.at[t],
-            recv_sem=q_recv.at[t],
+            src_ref=queries_ref.at[:, q_lanes(th, j)],
+            dst_ref=qbuf.at[j, pl.ds(start, small)],
+            send_sem=q_send.at[j, t],
+            recv_sem=q_recv.at[j, t],
             device_id=(patch_of(z, tx, core), th),
             device_id_type=MESH,
         )
 
-    q_self = pltpu.make_async_copy(
-        queries_ref.at[:, pl.ds(pl.multiple_of(head * width, LANES), width)],
-        qbuf.at[pl.ds(pl.multiple_of(head * small, small), small), :],
-        q_recv.at[0],
-    )
-    q_self.start()
-
-    @pl.loop(1, 2 * nh)
-    def _(t):
-        q_copy(t).start()
+    def q_self(j):
+        return pltpu.make_async_copy(
+            queries_ref.at[:, q_lanes(head, j)],
+            qbuf.at[j, pl.ds(pl.multiple_of(head * small, small), small)],
+            q_recv.at[j, 0],
+        )
+
+    def q_start(j):
+        q_self(j).start()
+
+        @pl.loop(1, 2 * nh)
+        def _(t):
+            q_copy(t, j).start()
+
+    def q_cross(j):
+        return pltpu.make_async_remote_copy(
+            src_ref=qbuf.at[j, pl.ds(0, 2 * rows)],
+            dst_ref=qbuf.at[j, pl.ds(2 * rows, 2 * rows)],
+            send_sem=qc_sem.at[0, j],
+            recv_sem=qc_sem.at[1, j],
+            device_id=partner,
+            device_id_type=MESH,
+        )
+
+    def q_arrive(j):
+        q_self(j).wait()
+
+        @pl.loop(1, 2 * nh)
+        def _(t):
+            q_copy(t, j).wait_recv()
+
+        q_cross(j).start()
+
+    mid = nz // 2
+    slow = z // mid
+    fast = 1 - slow
+    to_end = z + slow * (nz - 1 - 2 * z)
+
+    def source(s, way):
+        return lax.rem(z + 2 * nz - (1 - 2 * way) * s, nz)
 
     def ring_copy(j, s, way):
-        slot = lax.rem(z + nz - s, nz) if way == 0 else lax.rem(z + s, nz)
-        ref = codes.at[j, slot]
-        if s == nz // 2 - 1:
-            ref = ref.at[pl.ds(way * half, half)]
+        ref = codes.at[j, source(s, way)]
         return pltpu.make_async_remote_copy(
             src_ref=ref,
             dst_ref=ref,
             send_sem=ring_send.at[j, s, way],
             recv_sem=ring_recv.at[j, s, way],
-            device_id=right if way == 0 else left,
+            device_id=(patch_of(lax.rem(z + nz + 1 - 2 * way, nz), xh, core), head),
             device_id_type=MESH,
         )
 
+    def last_hop(way):
+        if way is fast:
+            return z * (nz - 1 - z) > 0
+        return (z - mid) * (z - mid + 1) == 0
+
+    def pass_on(j, s, way):
+        ring_copy(j, s, way).wait_recv()
+        if s < mid - 2:
+            ring_copy(j, s + 1, way).start()
+        elif s == mid - 2:
+
+            @pl.when(last_hop(way))
+            def _():
+                ring_copy(j, s + 1, way).start()
+
     def old_rows(j, side, patch_id):
-        return stale[2 * j + side][owner_ref[patch_id]].astype(F32)
+        return stale[2 * j + side][owner_smem[patch_id]].astype(F32)
 
     def encode(j):
         lanes = slice(j * LANES, (j + 1) * LANES)
@@ -186,7 +240,7 @@
 
     def decode(j, slot, chunk, side):
         patch_id = patch_of(slot, xh, core)
-        count = step_ref[patch_id].astype(F32)
+        count = step_smem[patch_id].astype(F32)
         pairs = count * (count - 1.0)
         keep = 0.5 - 0.25 * count + 0.0625 * pairs - (pairs * (count - 2.0)) * (1 / 6) * 0.0625
         blend = 1.0 - keep
@@ -201,18 +255,24 @@
             own_values[j, at, :LANES] = new_v
 
     def arrive(j, s):
-        for way in range(2):
-            ring_copy(j, s, way).wait_recv()
-        if s < nz // 2 - 1:
-            for way in range(2):
-                ring_copy(j, s + 1, way).start()
-            decode(j, lax.rem(z + nz - 1 - s, nz), s, 1)
-            decode(j, lax.rem(z + 1 + s, nz), s + 1, 0)
-        else:
-            decode(j, lax.rem(z + nz // 2, nz), s, 1)
+        pass_on(j, s, fast)
+        if s < mid - 1:
+
+            @pl.when(to_end > s)
+            def _():
+                pass_on(j, s, slow)
+
+        decode(j, source(s + 1, fast), s, 1 if s == 0 else 0)
+        if s > 0:
+
+            @pl.when(to_end <= s - 1)
+            def _():
+                pass_on(j, s - 1, slow)
+
+            decode(j, source(s, slow), s, 1)
 
     def part(j, at, k, v, first):
-        q = qbuf[at, j * LANES : (j + 1) * LANES]
+        q = qbuf[j, at]
         scores = across(q, k)
         top = jnp.max(scores, axis=1, keepdims=True)
         if first:
@@ -293,99 +353,101 @@
             other = got_out[j, at].astype(F32)
             other_level = unpack(got_stat[j, g : g + 1])
             mixed = mix(result, level, other, other_level)
-            sum_out[at, j * LANES : (j + 1) * LANES] = mixed.astype(BF16)
+            sum_out[j, at] = mixed.astype(BF16)
             top = jnp.maximum(level, other_level)
             low = jnp.minimum(level, other_level)
             joint = top + jnp.log(1.0 + jnp.exp2(low - top)) * LOG2E
             sum_stat[g, j : j + 1] = pack(joint)
 
-    def final_refs(t, th):
-        src = sum_out.at[
-            pl.ds(pl.multiple_of((t // nh) * rows + th * small, small), small), :
-        ]
-        dst = final_out.at[t // nh, :, pl.ds(pl.multiple_of(head * width, LANES), width)]
-        stat_src = sum_stat.at[(t // nh) * groups + th // per_group]
-        stat_dst = final_stat.at[t // nh, head]
-        return (src, dst), (stat_src, stat_dst)
-
-    def final_copy(t, which):
+    def final_refs(t, th, j):
+        if j == heads:
+            src = sum_stat.at[(t // nh) * groups + th // per_group]
+            return src, final_stat.at[t // nh, head]
+        start = pl.multiple_of((t // nh) * rows + th * small, small)
+        return sum_out.at[j, pl.ds(start, small)], final_out.at[t // nh, head, j]
+
+    def final_copy(t, j):
         tx, th = plane(t)
-        src, dst = final_refs(t, th)[which]
+        src, dst = final_refs(t, th, j)
         return pltpu.make_async_remote_copy(
             src_ref=src,
             dst_ref=dst,
-            send_sem=final_send.at[which, t],
-            recv_sem=final_recv.at[which, t],
+            send_sem=final_send.at[j, t],
+            recv_sem=final_recv.at[j, t],
             device_id=(patch_of(z, tx, core), th),
             device_id_type=MESH,
         )
 
-    for load in loads[:2]:
-        load.wait()
+    def final_self(j):
+        src, dst = final_refs(0, head, j)
+        return pltpu.make_async_copy(src, dst, final_recv.at[j, 0])
+
+    def final_start(j):
+        final_self(j).start()
+
+        @pl.loop(1, 2 * nh)
+        def _(t):
+            final_copy(t, j).start()
+
     for j in range(heads):
+        q_start(j)
+        if j == 0:
+            for load in loads[:2]:
+                load.wait()
         loads[2 + 2 * j].wait()
         loads[3 + 2 * j].wait()
         encode(j)
 
-    q_self.wait()
-
-    @pl.loop(1, 2 * nh)
-    def _(t):
-        q_copy(t).wait_recv()
-
-    q_cross = pltpu.make_async_remote_copy(
-        src_ref=qbuf.at[pl.ds(0, 2 * rows)],
-        dst_ref=qbuf.at[pl.ds(2 * rows, 2 * rows)],
-        send_sem=qc_sem.at[0],
-        recv_sem=qc_sem.at[1],
-        device_id=partner,
-        device_id_type=MESH,
-    )
-    q_cross.start()
-
+    ones = jnp.ones(values.shape[2:3] + (LANES,), BF16)
     for j in range(heads):
+        own_values[j, :, LANES:] = ones
+        for chunk in range(nz // 2):
+            values[j, chunk, :, LANES:] = ones
         own_keys[j, :rows] = fresh[0, :, j * LANES : (j + 1) * LANES]
         own_values[j, :rows, :LANES] = fresh[1, :, j * LANES : (j + 1) * LANES]
         decode(j, z, 0, 0)
-    for j in range(heads):
+    sum_stat[...] = jnp.zeros(sum_stat.shape, F32)
+
+    for j in range(min(2, heads)):
+        q_arrive(j)
         arrive(j, 0)
-    q_cross.wait_recv()
 
     steps = nz // 2
     items = [(s, j) for s in range(steps) for j in range(heads)]
-    seen = heads
+
+    def arrives_after(k):
+        if k < 2 * heads:
+            return k - heads + (1 if heads > 2 else 0)
+        return k - 2 if k <= 3 * heads else k - 1
+
     for i, (s, j) in enumerate(items):
-        ahead = 2 if s == 0 else 1
-        while seen <= i or (seen < i + ahead and seen < 2 * heads):
-            arrive(items[seen][1], items[seen][0])
-            seen += 1
+        if s == 0:
+            q_cross(j).wait_recv()
         attend(j, s)
+        if s == 0 and j + 2 < heads:
+            q_arrive(j + 2)
+            arrive(j + 2, 0)
         if s == steps - 1:
             share(j)
-
-    for j in range(heads):
+            if j == heads - 2:
+                for other in range(j):
+                    merge(other)
+                    final_start(other)
+        for k in range(heads, len(items)):
+            if arrives_after(k) == i:
+                arrive(items[k][1], items[k][0])
+    for j in range(max(heads - 2, 0), heads):
         merge(j)
-
-    (src, dst), (stat_src, stat_dst) = final_refs(0, head)
-    final_self = [
-        pltpu.make_async_copy(src, dst, final_recv.at[0, 0]),
-        pltpu.make_async_copy(stat_src, stat_dst, final_recv.at[1, 0]),
-    ]
-    for copy in final_self:
-        copy.start()
+        final_start(j)
+    final_start(heads)
+
+    for j in range(heads + 1):
+        final_self(j).wait()
 
     @pl.loop(1, 2 * nh)
     def _(t):
-        for which in range(2):
-            final_copy(t, which).start()
-
-    for copy in final_self:
-        copy.wait()
-
-    @pl.loop(1, 2 * nh)
-    def _(t):
-        for which in range(2):
-            final_copy(t, which).wait_recv()
+        for j in range(heads + 1):
+            final_copy(t, j).wait_recv()
 
     lane = lax.broadcasted_iota(jnp.int32, (small, LANES), 1)
     row = lax.broadcasted_iota(jnp.int32, (small, LANES), 0)
@@ -396,26 +458,33 @@
             jnp.where(mine, jnp.broadcast_to(line, (small, LANES)), 0.0), axis=1, keepdims=True
         )
 
-    @pl.loop(0, nh)
+    @pl.loop(0, nh, unroll=True)
     def _(g):
         for j in range(heads):
             lanes = pl.ds(pl.multiple_of((g * heads + j) * LANES, LANES), LANES)
-            results = [final_out[x, :, lanes].astype(F32) for x in range(2)]
+            results = [final_out[x, g, j].astype(F32) for x in range(2)]
             levels = [pick(final_stat[x, g, j : j + 1]) for x in range(2)]
             mixed = mix(results[0], levels[0], results[1], levels[1])
             out_ref[:, lanes] = mixed.astype(BF16)
 
     @pl.loop(1, 2 * nh)
     def _(t):
-        q_copy(t).wait_send()
-        for which in range(2):
-            final_copy(t, which).wait_send()
-
-    q_cross.wait_send()
+        for j in range(heads):
+            q_copy(t, j).wait_send()
+        for j in range(heads + 1):
+            final_copy(t, j).wait_send()
+
     for j in range(heads):
-        for s in range(steps):
+        q_cross(j).wait_send()
+        for s in range(steps - 1):
             for way in range(2):
                 ring_copy(j, s, way).wait_send()
+        for way in (fast, slow):
+
+            @pl.when(last_hop(way))
+            def _():
+                ring_copy(j, steps - 1, way).wait_send()
+
         for which in range(2):
             part_copy(j, which).wait_send()
 
@@ -439,15 +508,17 @@
         seq = stale_keys.shape[0]
         chunks = nz // 2
         groups = rows // LANES
-        smem = pl.BlockSpec(memory_space=pltpu.SMEM)
         hbm = pl.BlockSpec(memory_space=pl.ANY)
         vmem = pl.BlockSpec(memory_space=pltpu.VMEM)
         dma = pltpu.SemaphoreType.DMA
         scratch = [
+            pltpu.SMEM(owner_table.shape, jnp.int32),
+            pltpu.SMEM(step_counter.shape, jnp.int32),
+            pltpu.VMEM((2, heads) + key_basis.shape[:0:-1], BF16),
             [pltpu.VMEM((seq // rows, rows, LANES), BF16) for _ in range(2 * heads)],
             pltpu.VMEM((2, rows, width), BF16),
             pltpu.VMEM((heads, LANES, 2 * LANES), BF16),
-            pltpu.VMEM((4 * rows, width), BF16),
+            pltpu.VMEM((heads, 4 * rows, LANES), BF16),
             pltpu.VMEM((heads, nz, rows, LANES), BF16),
             pltpu.VMEM((heads, chunks, 2 * rows, LANES), BF16),
             pltpu.VMEM((heads, chunks, 2 * rows, 2 * LANES), BF16),
@@ -459,29 +530,29 @@
             pltpu.VMEM((heads, 8, LANES), F32),
             pltpu.VMEM((heads, 2 * rows, LANES), BF16),
             pltpu.VMEM((heads, 8, LANES), F32),
-            pltpu.VMEM((2 * rows, width), BF16),
+            pltpu.VMEM((heads, 2 * rows, LANES), BF16),
             pltpu.VMEM((2 * groups, 8, LANES), F32),
-            pltpu.VMEM((2, small, nh * width), BF16),
+            pltpu.VMEM((2, nh, heads, small, LANES), BF16),
             pltpu.VMEM((2, nh, 8, LANES), F32),
-            dma((2 + 2 * heads,)),
-            dma((2 * nh,)),
-            dma((2 * nh,)),
-            dma((2,)),
+            dma((6 + 2 * heads,)),
+            dma((heads, 2 * nh)),
+            dma((heads, 2 * nh)),
+            dma((2, heads)),
             dma((heads, chunks, 2)),
             dma((heads, chunks, 2)),
             dma((heads, 2)),
             dma((heads, 2)),
-            dma((2, 2 * nh)),
-            dma((2, 2 * nh)),
+            dma((heads + 1, 2 * nh)),
+            dma((heads + 1, 2 * nh)),
         ]
         return pl.pallas_call(
             functools.partial(kernel, (heads, nz, nh, rows)),
             out_shape=jax.ShapeDtypeStruct((small, nh * width), BF16),
-            in_specs=[smem, smem, hbm, hbm, hbm, hbm, hbm, vmem, vmem],
+            in_specs=[hbm] * 9,
             out_specs=vmem,
             scratch_shapes=scratch,
             compiler_params=pltpu.CompilerParams(
-                collective_id=0, has_side_effects=True, vmem_limit_bytes=48 << 20
+                collective_id=0, has_side_effects=True, vmem_limit_bytes=62 << 20
             ),
             name="patch_attention",
         )(

time: 58.4 us -> 47.9 us (0.82)
  Pallas kernels: 51.8 us -> 46.2 us
  local copies, waits for them, and re-layouts: 6.36 us -> 1.62 us
    pallas_call x1, Pallas kernels: 51.8 us -> 46.2 us  [local(): pl.pallas_call(functools.partial(kernel, (heads, nz, nh, rows)), out_shap...]
    unnamed x15 -> x1, local copies, waits for them, and re-layouts: 6.36 us -> 1.62 us
where the time goes in v2:
time: 47.9 us; the launch traced here: 47.8 us
  Pallas kernels  46.2 us (96%)
  local copies, waits for them, and re-layouts  1.62 us (3%)
    pallas_call x1, Pallas kernels, local(): pl.pallas_call(functools.partial(kernel, (heads, nz, nh, rows)), out_shap...  46.2 us
    unnamed x1, local copies, waits for them, and re-layouts  1.62 us

profile of v2, /device:TPU:1, one launch (start us, length us, event | category | flops | bytes accessed | tf_op | source)
XLA Modules:
  0.0 47.8 jit_solution(11150197980069761843)
XLA Ops:
  0.0 46.2 %patch_attention.1 = bf16[32,3072]{1,0:T(8,128)(2,1)} custom-call(s32[32]{0:T(128)} %owner_ref.1, s32[32]{0:T(128)} %step_ref.1, bf16[32,3072]{1,0:T(8,128)(2,1)} %queries_ref.1, bf16[256,384]{1,0:T(8,128)(2,1)} %fresh_k_ref.1, bf16[256,384]{1,0:T(8,128)(2,1)} %fresh_v_ref.1, bf16[32,256,384]{2,1,0:T(8,128)(2,1)} %bitcast.4, bf16[32,256,384]{2,1,0:T(8,128)(2,1)} %bitcast.5, ...), custom_call_target="tpu_custom_call" | custom-call | tf_op jit(solution)/shard_map/patch_attention/pallas_call | solution.py:548
  46.2 1.6 %copy.11 = bf16[32,3072]{1,0:T(8,128)(2,1)} copy(bf16[32,3072]{1,0:T(8,128)(2,1)} %patch_attention.1) | data formatting | bytes 393216

commit v3 on v2

--- a/solution.py
+++ b/solution.py
@@ -271,31 +271,54 @@
 
             decode(j, source(s, slow), s, 1)
 
-    def part(j, at, k, v, first):
-        q = qbuf[j, at]
-        scores = across(q, k)
-        top = jnp.max(scores, axis=1, keepdims=True)
-        if first:
-            now = jnp.broadcast_to(top, (q.shape[0], LANES))
-        else:
-            before = best[j, at]
-            now = jnp.maximum(before, top)
-        weights = jnp.exp2(scores * scale - now[:, :1] * scale).astype(BF16)
-        added = jnp.dot(weights, v, preferred_element_type=F32)
-        if first:
-            acc[j, at] = added
-        else:
-            factor = jnp.exp2((before - now) * scale)
-            acc[j, at, :LANES] = acc[j, at, :LANES] * factor + added[:, :LANES]
-            acc[j, at, LANES:] = acc[j, at, LANES:] * factor + added[:, LANES:]
-        best[j, at] = now
-
     def attend(j, chunk):
         if chunk == 0:
-            part(j, slice(0, rows), own_keys[j], own_values[j], True)
-            part(j, slice(rows, 4 * rows), keys[j, 0], values[j, 0], True)
+            tiles = (
+                (slice(0, rows), own_keys[j], own_values[j]),
+                (slice(rows, 5 * rows // 2), keys[j, 0], values[j, 0]),
+                (slice(5 * rows // 2, 4 * rows), keys[j, 0], values[j, 0]),
+            )
         else:
-            part(j, slice(0, 4 * rows), keys[j, chunk], values[j, chunk], False)
+            tiles = (
+                (slice(0, 2 * rows), keys[j, chunk], values[j, chunk]),
+                (slice(2 * rows, 4 * rows), keys[j, chunk], values[j, chunk]),
+            )
+
+        def score(t):
+            at, k, _ = tiles[t]
+            return across(qbuf[j, at], k)
+
+        def weigh(t, scores):
+            at = tiles[t][0]
+            now = jnp.max(scores, axis=1, keepdims=True)
+            factor = None
+            if chunk == 0:
+                now = jnp.broadcast_to(now, (scores.shape[0], LANES))
+            else:
+                before = best[j, at]
+                now = jnp.maximum(before, now)
+                factor = jnp.exp2((before - now) * scale)
+            best[j, at] = now
+            return jnp.exp2(scores * scale - now[:, :1] * scale).astype(BF16), factor
+
+        def add(t, weights, factor):
+            at, _, v = tiles[t]
+            added = jnp.dot(weights, v, preferred_element_type=F32)
+            if chunk == 0:
+                acc[j, at] = added
+            else:
+                acc[j, at, :LANES] = acc[j, at, :LANES] * factor + added[:, :LANES]
+                acc[j, at, LANES:] = acc[j, at, LANES:] * factor + added[:, LANES:]
+
+        scores = score(0)
+        ready = None
+        for t in range(len(tiles)):
+            following = score(t + 1) if t + 1 < len(tiles) else None
+            weighed = weigh(t, scores)
+            if ready is not None:
+                add(t - 1, *ready)
+            ready, scores = weighed, following
+        add(len(tiles) - 1, *ready)
 
     row_id = lax.broadcasted_iota(jnp.int32, (LANES, LANES), 0)
     lane_id = lax.broadcasted_iota(jnp.int32, (LANES, LANES), 1)
@@ -340,8 +363,10 @@
         for which in range(2):
             part_copy(j, which).start()
 
-    def mix(result_a, level_a, result_b, level_b):
-        share_a = 1.0 / (1.0 + jnp.exp2(level_b - level_a))
+    def share_of(level_a, level_b):
+        return 1.0 / (1.0 + jnp.exp2(level_b - level_a))
+
+    def mix(result_a, result_b, share_a):
         return result_a * share_a + result_b * (1.0 - share_a)
 
     def merge(j):
@@ -352,7 +377,7 @@
             result, level = local_result(j, pl.ds(g * LANES, LANES))
             other = got_out[j, at].astype(F32)
             other_level = unpack(got_stat[j, g : g + 1])
-            mixed = mix(result, level, other, other_level)
+            mixed = mix(result, other, share_of(level, other_level))
             sum_out[j, at] = mixed.astype(BF16)
             top = jnp.maximum(level, other_level)
             low = jnp.minimum(level, other_level)
@@ -408,25 +433,22 @@
         decode(j, z, 0, 0)
     sum_stat[...] = jnp.zeros(sum_stat.shape, F32)
 
-    for j in range(min(2, heads)):
+    for j in range(heads):
+        arrive(j, 0)
         q_arrive(j)
-        arrive(j, 0)
 
     steps = nz // 2
     items = [(s, j) for s in range(steps) for j in range(heads)]
 
     def arrives_after(k):
-        if k < 2 * heads:
-            return k - heads + (1 if heads > 2 else 0)
-        return k - 2 if k <= 3 * heads else k - 1
+        if k < 3 * heads:
+            return k - heads
+        return k - 2 if k == 3 * heads else k - 1
 
     for i, (s, j) in enumerate(items):
         if s == 0:
             q_cross(j).wait_recv()
         attend(j, s)
-        if s == 0 and j + 2 < heads:
-            q_arrive(j + 2)
-            arrive(j + 2, 0)
         if s == steps - 1:
             share(j)
             if j == heads - 2:
@@ -460,11 +482,11 @@
 
     @pl.loop(0, nh, unroll=True)
     def _(g):
+        shares = share_of(final_stat[0, g], final_stat[1, g])
         for j in range(heads):
             lanes = pl.ds(pl.multiple_of((g * heads + j) * LANES, LANES), LANES)
             results = [final_out[x, g, j].astype(F32) for x in range(2)]
-            levels = [pick(final_stat[x, g, j : j + 1]) for x in range(2)]
-            mixed = mix(results[0], levels[0], results[1], levels[1])
+            mixed = mix(results[0], results[1], pick(shares[j : j + 1]))
             out_ref[:, lanes] = mixed.astype(BF16)
 
     @pl.loop(1, 2 * nh)

time: 47.9 us -> 45.5 us (0.950)
  Pallas kernels: 46.2 us -> 43.8 us
    pallas_call x1, Pallas kernels: 46.2 us -> 43.8 us  [local(): pl.pallas_call(functools.partial(kernel, (heads, nz, nh, rows)), out_shap...]
where the time goes in v3:
time: 45.5 us; the launch traced here: 45.4 us
  Pallas kernels  43.8 us (96%)
  local copies, waits for them, and re-layouts  1.62 us (4%)
    pallas_call x1, Pallas kernels, local(): pl.pallas_call(functools.partial(kernel, (heads, nz, nh, rows)), out_shap...  43.8 us
    unnamed x1, local copies, waits for them, and re-layouts  1.62 us

profile of v3, /device:TPU:1, one launch (start us, length us, event | category | flops | bytes accessed | tf_op | source)
XLA Modules:
  0.0 45.4 jit_solution(4753038935156382359)
XLA Ops:
  0.0 43.8 %patch_attention.1 = bf16[32,3072]{1,0:T(8,128)(2,1)} custom-call(s32[32]{0:T(128)} %owner_ref.1, s32[32]{0:T(128)} %step_ref.1, bf16[32,3072]{1,0:T(8,128)(2,1)} %queries_ref.1, bf16[256,384]{1,0:T(8,128)(2,1)} %fresh_k_ref.1, bf16[256,384]{1,0:T(8,128)(2,1)} %fresh_v_ref.1, bf16[32,256,384]{2,1,0:T(8,128)(2,1)} %bitcast.4, bf16[32,256,384]{2,1,0:T(8,128)(2,1)} %bitcast.5, ...), custom_call_target="tpu_custom_call" | custom-call | tf_op jit(solution)/shard_map/patch_attention/pallas_call | solution.py:570
  43.8 1.6 %copy.11 = bf16[32,3072]{1,0:T(8,128)(2,1)} copy(bf16[32,3072]{1,0:T(8,128)(2,1)} %patch_attention.1) | data formatting | bytes 393216

commit v4 on v3

--- a/solution.py
+++ b/solution.py
@@ -262,13 +262,14 @@
             def _():
                 pass_on(j, s, slow)
 
-        decode(j, source(s + 1, fast), s, 1 if s == 0 else 0)
         if s > 0:
 
             @pl.when(to_end <= s - 1)
             def _():
                 pass_on(j, s - 1, slow)
 
+        decode(j, source(s + 1, fast), s, 1 if s == 0 else 0)
+        if s > 0:
             decode(j, source(s, slow), s, 1)
 
     def attend(j, chunk):

time: 45.5 us -> 44.8 us (0.985)
  Pallas kernels: 43.8 us -> 43 us
    pallas_call x1, Pallas kernels: 43.8 us -> 43 us  [local(): pl.pallas_call(functools.partial(kernel, (heads, nz, nh, rows)), out_shap...]
where the time goes in v4:
time: 44.8 us; the launch traced here: 44.7 us
  Pallas kernels  43 us (96%)
  local copies, waits for them, and re-layouts  1.62 us (4%)
    pallas_call x1, Pallas kernels, local(): pl.pallas_call(functools.partial(kernel, (heads, nz, nh, rows)), out_shap...  43 us
    unnamed x1, local copies, waits for them, and re-layouts  1.62 us

profile of v4, /device:TPU:1, one launch (start us, length us, event | category | flops | bytes accessed | tf_op | source)
XLA Modules:
  0.0 44.7 jit_solution(2176617312129925076)
XLA Ops:
  0.0 43.0 %patch_attention.1 = bf16[32,3072]{1,0:T(8,128)(2,1)} custom-call(s32[32]{0:T(128)} %owner_ref.1, s32[32]{0:T(128)} %step_ref.1, bf16[32,3072]{1,0:T(8,128)(2,1)} %queries_ref.1, bf16[256,384]{1,0:T(8,128)(2,1)} %fresh_k_ref.1, bf16[256,384]{1,0:T(8,128)(2,1)} %fresh_v_ref.1, bf16[32,256,384]{2,1,0:T(8,128)(2,1)} %bitcast.4, bf16[32,256,384]{2,1,0:T(8,128)(2,1)} %bitcast.5, ...), custom_call_target="tpu_custom_call" | custom-call | tf_op jit(solution)/shard_map/patch_attention/pallas_call | solution.py:571
  43.0 1.6 %copy.11 = bf16[32,3072]{1,0:T(8,128)(2,1)} copy(bf16[32,3072]{1,0:T(8,128)(2,1)} %patch_attention.1) | data formatting | bytes 393216
